TPU v7x, 32 devices: a whole 2x2x4 slice. The times are simulated.
32 devices in a mesh: group: 2 (over x), date: 16 (over z, y, core).
Axes of the slice: x: 2, y: 2, z: 4, core: 2. Of those that a mesh axis runs over, the one named last changes fastest.
Arguments:
- salvo_records: bfloat16 [32, 3, 2, 13, 1024], P(('group', 'date')), parts along dimension 0, may hold values from -6 to 6
- stencil_weights: bfloat16 [32, 3, 8], P(('group', 'date')), parts along dimension 0, may hold values from -2 to 2
- zone_drifts: int32 [32, 3], P(('group', 'date')), parts along dimension 0, may hold values from -16 to 16
- seam_sweeps: int32 [32, 2], P(('group', 'date')), parts along dimension 0, may hold values from 1 to 2
- prior_sweeps: int32 [32], P(('group', 'date')), parts along dimension 0, may hold values from 0 to 1
- viewing_frames: int32 [512, 128], P(('group', 'date')), parts along dimension 0, may hold values from 0 to 4095, as said below
Outputs:
- filtered: bfloat16 [32, 2, 32, 1024], P(('group', 'date')), parts along dimension 0
There are 2 independent parts, one for each index of `group`. A program takes and returns all parts, laid end to end along the dimension named above; each array names one. Nothing has to cross between parts.
Inputs may be any that keep to these rules, and one draw needn't show every extreme that they name: `viewing_frames`: window w belongs to ground block g = w // 16 and names pixels line-major among 4 lines of 1024 cells: local line 0 is the line above the block, lines 1 .. 2 the block, line 3 the line below. The first block never names local line 0, the last block never names local line 3.
All inputs are finite; a program needn't handle non-finite values.
Results may differ from a plain program's by a relative error of at most 0.019.
Values may be sent and summed in bfloat16 or wider, within the bound.
A program may use at most 64 MiB of HBM per device.

v0:
```python
import math

import jax
import jax.numpy as jnp
from jax import lax
from jax.sharding import PartitionSpec as P

LB = 2
SALVO_TALLY = 3
STENCIL_WEIGHTS = 8
LOOKS = 128
ITERS = 8
PATCH = 32


EPSILON = 1e-06
SHRINK = 0.05


def padded(block, sides, width):
    for axis, dim in sides:
        count = lax.axis_size(axis)
        forward = [(i, i + 1) for i in range(count - 1)]
        backward = [(target, source) for source, target in forward]
        low = lax.ppermute(
            lax.slice_in_dim(block, block.shape[dim] - width, None, axis=dim), axis, forward
        )
        high = lax.ppermute(lax.slice_in_dim(block, 0, width, axis=dim), axis, backward)
        block = jnp.concatenate([low, block, high], axis=dim)
    return block


def regridding_tableau(tap_row, offset, distance_readings):
    rows = lax.broadcasted_iota(jnp.int32, (distance_readings, distance_readings), 0)
    downward_entry_list = lax.broadcasted_iota(jnp.int32, (distance_readings, distance_readings), 1)
    distance = rows - downward_entry_list - offset + (STENCIL_WEIGHTS // 2 - 1)
    matrix = jnp.zeros((distance_readings, distance_readings), jnp.bfloat16)
    for tap_index in range(STENCIL_WEIGHTS):
        matrix = jnp.where(distance == tap_index, tap_row[tap_index], matrix)
    return matrix


def seam_lone_capture(
    piled_salvos, stencil_weight_table, distance_drifts, joint_sweep, opening_salvo, sweep_labels
):
    distance_readings = piled_salvos.shape[-1]
    sweeps_each_salvo = piled_salvos.shape[2]
    regridding_zones = jnp.stack(
        [
            regridding_tableau(
                stencil_weight_table[salvo_label], distance_drifts[salvo_label], distance_readings
            )
            for salvo_label in range(SALVO_TALLY)
        ]
    )
    regridded_salvos = jnp.einsum(
        "bndo,bot->bndt", piled_salvos, regridding_zones, preferred_element_type=jnp.float32
    ).astype(jnp.bfloat16)
    sweep_spacing = sweeps_each_salvo - joint_sweep
    salvo_beginnings = (
        jnp.concatenate([jnp.zeros((1,), jnp.int32), jnp.cumsum(sweep_spacing)]) - opening_salvo
    )
    flight_sweep_slot = lax.broadcasted_iota(jnp.int32, (sweep_labels, sweeps_each_salvo), 0)
    sweep_slot = lax.broadcasted_iota(jnp.int32, (sweep_labels, sweeps_each_salvo), 1)
    downward_entry_list = []
    for salvo_label in range(SALVO_TALLY):
        seam_ramp = jnp.ones((sweep_labels, sweeps_each_salvo), jnp.float32)
        if salvo_label > 0:
            upward_ramp = (flight_sweep_slot - salvo_beginnings[salvo_label] + 1).astype(
                jnp.float32
            ) / (joint_sweep[salvo_label - 1] + 1).astype(jnp.float32)
            seam_ramp = seam_ramp * jnp.clip(upward_ramp, 0.0, 1.0)
        if salvo_label < SALVO_TALLY - 1:
            downward_ramp = (
                salvo_beginnings[salvo_label] + sweeps_each_salvo - flight_sweep_slot
            ).astype(jnp.float32) / (joint_sweep[salvo_label] + 1).astype(jnp.float32)
            seam_ramp = seam_ramp * jnp.clip(downward_ramp, 0.0, 1.0)
        downward_entry_list.append(
            jnp.where(
                flight_sweep_slot == salvo_beginnings[salvo_label] + sweep_slot, seam_ramp, 0.0
            ).astype(jnp.bfloat16)
        )
    sweep_target_slot = jnp.stack(downward_entry_list, axis=1)
    return jnp.einsum(
        "tzg,zugi->uti", sweep_target_slot, regridded_salvos, preferred_element_type=jnp.float32
    ).astype(jnp.bfloat16)


def coupling_frames(readings, native_picture_elements):
    sample_real = readings[:, 0]
    sample_imaginary = readings[:, 1]

    def pair(left, right):
        return jnp.einsum("dwm,ewm->wde", left, right, preferred_element_type=jnp.float32)

    inverse_looks = 1.0 / LOOKS
    covariance_real = (
        pair(sample_real, sample_real) + pair(sample_imaginary, sample_imaginary)
    ) * inverse_looks
    mixed = pair(sample_imaginary, sample_real)
    covariance_imaginary = (mixed - jnp.swapaxes(mixed, 1, 2)) * inverse_looks
    dates = readings.shape[0]
    inverse_root = lax.rsqrt(jnp.diagonal(covariance_real, axis1=1, axis2=2) + EPSILON)
    outer = inverse_root[:, :, None] * inverse_root[:, None, :]
    identity = jnp.eye(dates, dtype=jnp.float32)
    coherence_real = (1.0 - SHRINK) * covariance_real * outer + SHRINK * identity
    coherence_imaginary = (1.0 - SHRINK) * covariance_imaginary * outer
    vector_real = jnp.ones(inverse_root.shape, jnp.float32)
    vector_imaginary = jnp.zeros(inverse_root.shape, jnp.float32)

    def apply_matrix(matrix, vector):
        return jnp.einsum("wde,we->wd", matrix, vector, precision=lax.Precision.HIGHEST)

    for iteration in range(ITERS):
        image_real = apply_matrix(coherence_real, vector_real) - apply_matrix(
            coherence_imaginary, vector_imaginary
        )
        image_imaginary = apply_matrix(coherence_real, vector_imaginary) + apply_matrix(
            coherence_imaginary, vector_real
        )
        factor = lax.rsqrt(
            jnp.mean(
                image_real * image_real + image_imaginary * image_imaginary, axis=1, keepdims=True
            )
            + EPSILON
        )
        vector_real = image_real * factor
        vector_imaginary = image_imaginary * factor
    coupled_result = jnp.stack([vector_real, vector_imaginary]).astype(jnp.bfloat16)

    def project(history, pixels):
        return jnp.einsum("wd,dwm->wm", history, pixels, preferred_element_type=jnp.float32)

    scaling = 1.0 / math.sqrt(dates)
    own_real = native_picture_elements[:, 0]
    own_imaginary = native_picture_elements[:, 1]
    compressed_real = (
        project(coupled_result[0], own_real) + project(coupled_result[1], own_imaginary)
    ) * scaling
    compressed_imaginary = (
        project(coupled_result[0], own_imaginary) - project(coupled_result[1], own_real)
    ) * scaling
    condensed_result = jnp.stack([compressed_real, compressed_imaginary]).astype(jnp.bfloat16)
    return (condensed_result, coupled_result)


def dft_tables(length, span):
    first = lax.broadcasted_iota(jnp.int32, (span, span), 0)
    second = lax.broadcasted_iota(jnp.int32, (span, span), 1)
    product = first % length * (second % length) % length
    angle = product.astype(jnp.float32) * (2.0 * math.pi / length)
    inside = first // length == second // length
    cosine = jnp.where(inside, jnp.cos(angle), 0.0).astype(jnp.bfloat16)
    sine = jnp.where(inside, jnp.sin(angle), 0.0).astype(jnp.bfloat16)
    return (cosine, sine)


def goldstein(rebuilt):
    sweep_labels = rebuilt.shape[1]
    distance_readings = rebuilt.shape[2]
    range_cos, range_sin = dft_tables(PATCH, 128)
    line_cos, line_sin = dft_tables(PATCH, PATCH)

    def across(matrix, table):
        return jnp.dot(matrix.reshape(-1, 128), table, preferred_element_type=jnp.float32).reshape(
            sweep_labels, distance_readings
        )

    def along(table, matrix):
        return jnp.einsum(
            "kn,pnr->pkr",
            table,
            matrix.reshape(sweep_labels // PATCH, PATCH, distance_readings),
            preferred_element_type=jnp.float32,
        )

    real_in = rebuilt[0]
    imaginary_in = rebuilt[1]
    first_real = (across(real_in, range_cos) + across(imaginary_in, range_sin)).astype(jnp.bfloat16)
    first_imaginary = (across(imaginary_in, range_cos) - across(real_in, range_sin)).astype(
        jnp.bfloat16
    )
    spectrum_real = along(line_cos, first_real) + along(line_sin, first_imaginary)
    spectrum_imaginary = along(line_cos, first_imaginary) - along(line_sin, first_real)
    power = spectrum_real * spectrum_real + spectrum_imaginary * spectrum_imaginary
    patch_total = (
        jnp.sum(power, axis=1)
        .reshape(sweep_labels // PATCH, distance_readings // PATCH, PATCH)
        .sum(axis=2)
    )
    patch_mean = jnp.repeat(patch_total / (PATCH * PATCH), PATCH, axis=1)[:, None, :]
    seam_ramp = jnp.sqrt(jnp.sqrt(power / (patch_mean + EPSILON)))
    weighted_real = (spectrum_real * seam_ramp).astype(jnp.bfloat16)
    weighted_imaginary = (spectrum_imaginary * seam_ramp).astype(jnp.bfloat16)
    back_real = (along(line_cos, weighted_real) - along(line_sin, weighted_imaginary)).astype(
        jnp.bfloat16
    )
    back_imaginary = (along(line_cos, weighted_imaginary) + along(line_sin, weighted_real)).astype(
        jnp.bfloat16
    )
    scaling = 1.0 / (PATCH * PATCH)
    out_real = (
        (across(back_real, range_cos) - across(back_imaginary, range_sin)) * scaling
    ).astype(jnp.bfloat16)
    out_imaginary = (
        (across(back_imaginary, range_cos) + across(back_real, range_sin)) * scaling
    ).astype(jnp.bfloat16)
    return jnp.stack([out_real, out_imaginary])


def on_device(
    salvo_records, stencil_weights, zone_drifts, seam_sweeps, prior_sweeps, viewing_frames
):
    devices = lax.axis_size("date")
    sweep_labels = LB * devices
    seamed_picture = seam_lone_capture(
        salvo_records[0],
        stencil_weights[0],
        zone_drifts[0],
        seam_sweeps[0],
        prior_sweeps[0],
        sweep_labels,
    )
    distance_readings = seamed_picture.shape[2]
    ground = lax.all_to_all(seamed_picture[None], "date", split_axis=2, concat_axis=0, tiled=True)
    extended = padded(ground, (("date", 2),), 1)
    windows_here = viewing_frames.shape[0]
    flat = extended.reshape(devices, 2, (LB + 2) * distance_readings)
    readings = jnp.take(flat, viewing_frames.reshape(-1), axis=2).reshape(
        devices, 2, windows_here, LOOKS
    )
    native_picture_elements = extended[:, :, 1 : LB + 1].reshape(devices, 2, windows_here, LOOKS)
    condensed_result, coupled_result = coupling_frames(readings, native_picture_elements)
    history_real = coupled_result[0].astype(jnp.float32).T[:, :, None]
    history_imaginary = coupled_result[1].astype(jnp.float32).T[:, :, None]
    value_real = condensed_result[0].astype(jnp.float32)[None]
    value_imaginary = condensed_result[1].astype(jnp.float32)[None]
    rebuilt = jnp.stack(
        [
            value_real * history_real - value_imaginary * history_imaginary,
            value_real * history_imaginary + value_imaginary * history_real,
        ],
        axis=1,
    ).astype(jnp.bfloat16)
    rebuilt = rebuilt.reshape(devices, 2, LB, distance_readings)
    mine = lax.all_to_all(rebuilt, "date", split_axis=0, concat_axis=2, tiled=True)[0]
    return goldstein(mine)[None]


def solution(mesh):
    in_specs = (
        P(("group", "date"), None, None, None, None),
        P(("group", "date"), None, None),
        P(("group", "date"), None),
        P(("group", "date"), None),
        P(("group", "date")),
        P(("group", "date"), None),
    )
    out_specs = P(("group", "date"), None, None, None)
    return jax.shard_map(
        on_device, mesh=mesh, in_specs=in_specs, out_specs=out_specs, check_vma=False
    )
```

profile of v0, /device:TPU:0, one launch (start us, length us, event | category | flops | bytes accessed | tf_op | source)
XLA Modules:
  0.0 115.2 jit_solution(11993288917228165708)
XLA Ops:
  0.0 2.1 %fusion.145 = (bf16[1,1,1]{2,1,0:T(2,128)(2,1)}, bf16[1,1,1]{2,1,0:T(2,128)(2,1)}, bf16[1,1,1]{2,1,0:T(2,128)(2,1)}, bf16[1,1,1]{2,1,0:T(2,128)(2,1)}, bf16[1,1,...) fusion(bf16[1,3,8]{2,1,0:T(4,128)(2,1)} %param.7), kind=kLoop, calls=%fused_computation.249 | loop fusion | bytes 76 | tf_op jit(solution)/shard_map/slice | solution.py:39
  2.1 1.5 %fusion.146 = (bf16[1,1,1]{2,1,0:T(2,128)(2,1)}, bf16[1,1,1]{2,1,0:T(2,128)(2,1)}, bf16[1,1,1]{2,1,0:T(2,128)(2,1)}, bf16[1,1,1]{2,1,0:T(2,128)(2,1)}, bf16[1,1,1]{2,1,0:T(2,128)(2,1)}) fusion(bf16[1,3,8]{2,1,0:T(4,128)(2,1)} %param.7), kind=kLoop, calls=%fused_computation.250 | loop fusion | bytes 20 | tf_op jit(solution)/shard_map/slice | solution.py:39
  3.6 0.7 subtract_bitcast_fusion
  4.3 1.4 %fusion.148 = (s32[1,1]{1,0:T(1,128)}, s32[1,1]{1,0:T(1,128)}) fusion(s32[1,2]{1,0:T(1,128)} %param.9), kind=kLoop, calls=%fused_computation.252 | loop fusion | bytes 16 | tf_op jit(solution)/shard_map/slice | solution.py:76
  6.6 0.7 fusion.147
  7.2 0.6 iota_add_fusion.1
  9.0 0.7 iota_add_fusion.2
  9.7 1.4 %fusion.149 = (s32[1,1]{1,0:T(1,128)}, s32[1,1]{1,0:T(1,128)}, s32[1,1]{1,0:T(1,128)}) fusion(s32[1,3]{1,0:T(1,128)} %param.8), kind=kLoop, calls=%fused_computation.253 | loop fusion | bytes 24 | tf_op jit(solution)/shard_map/slice | solution.py:51
  12.3 0.7 iota_add_fusion
  13.0 1.2 %divide_clamp_fusion = (bf16[32]{0:T(256)(128)(2,1)S(1)}, bf16[32]{0:T(256)(128)(2,1)S(1)}) fusion(s32[]{:T(128)} %bitcast.37, f32[]{:T(128)} %bitcast.36, s32[]{:T(128)S(6)} %add.411, f32[]{:T(128)} %bitcast.34, s32[]{:T(128)} %bitcast.35), kind=kLoop, calls=%fused_computation.209 | loop fusion | flops 544 | bytes 148 | tf_op jit(solution)/shard_map/jit(clip)/min | solution.py:72
  14.5 9.4 %fusion.41 = bf16[1,1024,1024]{2,1,0:T(8,128)(2,1)} fusion(s32[]{:T(128)} %bitcast, bf16[]{:T(256)} %bitcast.8, bf16[]{:T(256)} %bitcast.7, bf16[]{:T(256)} %bitcast.6, bf16[]{:T(256)} %bitcast.5, bf16[]{:T(256)} %bitcast.4, bf16[]{:T(256)} %bitcast.3, bf16[]{:T(256)} %bitcast.2, bf16[]{:T(256)} %bitcast.1), kind=kLoop, calls=%fused_computation.48 | loop fusion | flops 19922944 | bytes 2097172 | tf_op jit(solution)/shard_map/jit(_where)/select_n | solution.py:39
  23.9 17.7 %fusion.25 = (bf16[1,1024,1024]{2,1,0:T(8,128)(2,1)S(1)}, bf16[1,1024,1024]{2,1,0:T(8,128)(2,1)}) fusion(s32[]{:T(128)} %bitcast.18, bf16[]{:T(256)} %bitcast.26, bf16[]{:T(256)} %bitcast.25, bf16[]{:T(256)} %bitcast.24, bf16[]{:T(256)} %bitcast.23, bf16[]{:T(256)} %bitcast.22, bf16[]{:T(256)} %bitcast.21, bf16[]{:T(256)} %bitcast.20, bf16[]{:T(256)} %bitcast.19, ...), kind=kLoop, calls=%fused_computation.32 | loop fusion | flops 38797312 | bytes 4194344 | tf_op jit(solution)/shard_map/jit(_where)/select_n | solution.py:39
  41.6 3.5 %fusion.52 = bf16[1,2,32,1024]{3,2,1,0:T(8,128)(2,1)S(1)} fusion(bf16[1,1024,1024]{2,1,0:T(8,128)(2,1)S(1)} %get-tuple-element.99, bf16[1,1024,1024]{2,1,0:T(8,128)(2,1)} %get-tuple-element.100, bf16[1,1024,1024]{2,1,0:T(8,128)(2,1)} %fusion.41, bf16[3,2,13,1024]{3,1,2,0:T(2,128)(2,1)S(1)} %bitcast.325, bf16[32,1,13]{0,2,1:T(8,128)(2,1)S(1)} %select_convert_fusion.4, ...), kind=kOutput, calls=%fused_computation.61 | convolution fusion | flops 187711936 | bytes 6584768 | tf_op jit(solution)/shard_map/tzg,zugi->uti/dot_general | solution.py:84
  45.1 0.8 copy.59
  45.9 7.4 %all-to-all-start = ((bf16[1,2,32,1024]{3,1,0,2:T(2,128)(2,1)}), bf16[1,2,32,1024]{3,1,0,2:T(2,128)(2,1)S(1)}, u32[]{:S(2)}, u32[]{:S(2)}) async-start(bf16[1,2,32,1024]{3,1,0,2:T(2,128)(2,1)} %copy.59), calls=%async_computation | async-start | bytes 262144 | tf_op jit(solution)/shard_map/all_to_all | solution.py:225
  53.4 7.8 %all-to-all-done = bf16[1,2,32,1024]{3,1,0,2:T(2,128)(2,1)S(1)} async-done(((bf16[1,2,32,1024]{3,1,0,2:T(2,128)(2,1)}), bf16[1,2,32,1024]{3,1,0,2:T(2,128)(2,1)S(1)}, u32[]{:S(2)}, u32[]{:S(2)}) %all-to-all-start) | async-done | bytes 131104 | tf_op jit(solution)/shard_map/all_to_all | solution.py:225
  61.3 1.3 %collective-permute-start = (bf16[16,2,1,1024]{3,0,2,1:T(8,128)(2,1)S(1)}, bf16[16,2,1,1024]{3,0,2,1:T(8,128)(2,1)S(1)}, u32[]{:S(2)}, u32[]{:S(2)}) collective-permute-start(bf16[16,2,1,1024]{3,0,2,1:T(8,128)(2,1)S(1)} %get-tuple-element.39), channel_id=1, source_target_pairs={{0,1},{1,2},{2,3},{3,4},{4,5},{5,6},{6,7},{7,8},{8,9},{9,10},{10,1... | collective-permute-start | bytes 196616 | tf_op jit(solution)/shard_map/ppermute | solution.py:25
  62.6 1.5 %collective-permute-start.1 = (bf16[16,2,1,1024]{3,0,2,1:T(8,128)(2,1)S(1)}, bf16[16,2,1,1024]{3,0,2,1:T(8,128)(2,1)S(1)}, u32[]{:S(2)}, u32[]{:S(2)}) collective-permute-start(bf16[16,2,1,1024]{3,0,2,1:T(8,128)(2,1)S(1)} %get-tuple-element.40), channel_id=1, source_target_pairs={{1,0},{2,1},{3,2},{4,3},{5,4},{6,5},{7,6},{8,7},{9,8},{10,9},{11,1... | collective-permute-start | bytes 196616 | tf_op jit(solution)/shard_map/ppermute | solution.py:28
  64.3 1.4 %collective-permute-done.1 = bf16[16,2,1,1024]{3,0,2,1:T(8,128)(2,1)S(1)} collective-permute-done((bf16[16,2,1,1024]{3,0,2,1:T(8,128)(2,1)S(1)}, bf16[16,2,1,1024]{3,0,2,1:T(8,128)(2,1)S(1)}, u32[]{:S(2)}, u32[]{:S(2)}) %collective-permute-start.1) | collective-permute-done | bytes 65568 | tf_op jit(solution)/shard_map/ppermute | solution.py:28
  65.8 1.5 %copy.61 = bf16[16,2,4,1024]{0,1,3,2:T(2,128)(2,1)S(1)} copy(bf16[16,2,4,1024]{3,0,2,1:T(8,128)(2,1)S(1)} %pad_maximum_fusion) | data formatting | bytes 524288 | tf_op jit(solution)/shard_map/concatenate | solution.py:29
  67.2 7.1 %gather_fusion = bf16[2048,16,2]{1,2,0:T(2,128)(2,1)S(1)} fusion(bf16[16,2,4096]{0,1,2:T(2,128)(2,1)S(1)} %bitcast.326, s32[2048]{0:T(1024)S(1)} %broadcast_clamp_fusion), kind=kCustom, calls=%fused_computation | custom fusion | bytes 270336 | tf_op jit(solution)/shard_map/jit(_take)/gather | solution.py:229
  74.3 0.7 copy.63
  75.6 0.6 gather_fusion.1
  77.6 0.4 fusion.139
  78.3 0.4 fusion.137
  79.3 0.4 fusion.135
  80.0 0.4 fusion.133
  81.0 0.4 fusion.131
  81.7 0.4 fusion.129
  82.7 0.4 fusion.127
  83.4 0.4 fusion.125
  84.5 0.4 fusion.123
  85.1 0.4 fusion.121
  86.2 0.4 fusion.119
  86.8 0.4 fusion.117
  88.5 0.4 fusion.113
  91.5 0.8 pad_maximum_fusion.1
  92.3 7.2 %all-to-all-start.1 = ((bf16[16,2,2,1024]{3,2,1,0:T(2,128)(2,1)}), bf16[16,2,2,1024]{3,2,1,0:T(2,128)(2,1)S(1)}, u32[]{:S(2)}, u32[]{:S(2)}) async-start(bf16[16,2,2,1024]{3,2,1,0:T(2,128)(2,1)} %pad_maximum_fusion.1), calls=%async_computation.1 | async-start | bytes 262144 | tf_op jit(solution)/shard_map/all_to_all | solution.py:246
  99.6 7.9 %all-to-all-done.1 = bf16[16,2,2,1024]{3,2,1,0:T(2,128)(2,1)S(1)} async-done(((bf16[16,2,2,1024]{3,2,1,0:T(2,128)(2,1)}), bf16[16,2,2,1024]{3,2,1,0:T(2,128)(2,1)S(1)}, u32[]{:S(2)}, u32[]{:S(2)}) %all-to-all-start.1) | async-done | bytes 131104 | tf_op jit(solution)/shard_map/all_to_all | solution.py:246
  107.7 0.5 fusion.105
  108.2 0.5 fusion.106
  108.6 0.5 fusion.60
  109.2 0.5 fusion.59
  112.2 0.5 fusion.104
  113.0 0.5 fusion.103
  113.5 0.5 fusion.57
  114.0 0.5 fusion.58
  114.5 0.7 maximum_bitcast_fusion.10
  (120 shorter events, 14.1 us)
Async XLA Ops:
  0.0 41.6 %copy-start = (bf16[1,3,2,13,1024]{4,2,3,1,0:T(2,128)(2,1)S(1)}, bf16[1,3,2,13,1024]{4,2,3,1,0:T(2,128)(2,1)}, u32[]{:S(2)}) copy-start(bf16[1,3,2,13,1024]{4,2,3,1,0:T(2,128)(2,1)} %param.6) | copy-start | bytes 479236
  41.6 11.8 %copy-start.1 = (s32[16,128]{1,0:T(8,128)S(1)}, s32[16,128]{1,0:T(8,128)}, u32[]{:S(2)}) copy-start(s32[16,128]{1,0:T(8,128)} %param.11) | copy-start | bytes 24580
  45.9 15.3 %all-to-all-start = ((bf16[1,2,32,1024]{3,1,0,2:T(2,128)(2,1)}), bf16[1,2,32,1024]{3,1,0,2:T(2,128)(2,1)S(1)}, u32[]{:S(2)}, u32[]{:S(2)}) async-start(bf16[1,2,32,1024]{3,1,0,2:T(2,128)(2,1)} %copy.59), calls=%async_computation | async-start | bytes 262144 | tf_op jit(solution)/shard_map/all_to_all | solution.py:225
  61.3 3.0 %collective-permute-start = (bf16[16,2,1,1024]{3,0,2,1:T(8,128)(2,1)S(1)}, bf16[16,2,1,1024]{3,0,2,1:T(8,128)(2,1)S(1)}, u32[]{:S(2)}, u32[]{:S(2)}) collective-permute-start(bf16[16,2,1,1024]{3,0,2,1:T(8,128)(2,1)S(1)} %get-tuple-element.39), channel_id=1, source_target_pairs={{0,1},{1,2},{2,3},{3,4},{4,5},{5,6},{6,7},{7,8},{8,9},{9,10},{10,1... | collective-permute-start | bytes 196616 | tf_op jit(solution)/shard_map/ppermute | solution.py:25
  62.6 3.1 %collective-permute-start.1 = (bf16[16,2,1,1024]{3,0,2,1:T(8,128)(2,1)S(1)}, bf16[16,2,1,1024]{3,0,2,1:T(8,128)(2,1)S(1)}, u32[]{:S(2)}, u32[]{:S(2)}) collective-permute-start(bf16[16,2,1,1024]{3,0,2,1:T(8,128)(2,1)S(1)} %get-tuple-element.40), channel_id=1, source_target_pairs={{1,0},{2,1},{3,2},{4,3},{5,4},{6,5},{7,6},{8,7},{9,8},{10,9},{11,1... | collective-permute-start | bytes 196616 | tf_op jit(solution)/shard_map/ppermute | solution.py:28
  92.3 15.2 %all-to-all-start.1 = ((bf16[16,2,2,1024]{3,2,1,0:T(2,128)(2,1)}), bf16[16,2,2,1024]{3,2,1,0:T(2,128)(2,1)S(1)}, u32[]{:S(2)}, u32[]{:S(2)}) async-start(bf16[16,2,2,1024]{3,2,1,0:T(2,128)(2,1)} %pad_maximum_fusion.1), calls=%async_computation.1 | async-start | bytes 262144 | tf_op jit(solution)/shard_map/all_to_all | solution.py:246
where the time goes:
time: 116 us; the launch traced here: 115 us
  other arithmetic  35.1 us (30%)
  matrix products  22.4 us (19%)
  local copies, waits for them, and re-layouts  19.4 us (17%)
  starting transfers between devices  17.4 us (15%)
  waiting for transfers between devices  17.1 us (15%)
  between operations  3.85 us (3%)
    select_n x2, other arithmetic, regridding_tableau(): matrix = jnp.where(distance == tap_index, tap_row[tap_index], matrix)  27.1 us
    dot_general x32, matrix products, apply_matrix(): jnp.einsum('wde,we->wd', matrix, vector, precision=lax.Precision.HIGHEST)  11.8 us
    all_to_all x1, waiting for transfers between devices, on_device(): lax.all_to_all(rebuilt, 'date', split_axis=0, concat_axis=2, tiled=True)[0]  7.89 us
    all_to_all x1, waiting for transfers between devices, on_device(): lax.all_to_all(seamed_picture[None], 'date', split_axis=2, concat_axis=0,...  7.82 us
    gather x2, local copies, waits for them, and re-layouts, on_device(): jnp.take(flat, viewing_frames.reshape(-1), axis=2)  7.75 us
    all_to_all x1, starting transfers between devices, on_device(): lax.all_to_all(seamed_picture[None], 'date', split_axis=2, concat_axis=0,...  7.39 us
    all_to_all x1, starting transfers between devices, on_device(): lax.all_to_all(rebuilt, 'date', split_axis=0, concat_axis=2, tiled=True)[0]  7.24 us
    dot_general x8, matrix products, across(): jnp.dot(matrix.reshape(-1, 128), table, preferred_element_type=jnp.float32)  3.81 us
  transfers between devices with their start and end apart: 4, of which 3 were waited for; matrix products, arithmetic and copies ran while one was open for 0% of the time, Pallas kernels for 0%

commit v1 on v0

v1 whole, which is shorter than its diff:
```python
import functools
import math

import jax
import jax.numpy as jnp
import ml_dtypes
import numpy as np
from jax import lax
from jax.experimental import pallas as pl
from jax.experimental.pallas import tpu as pltpu

LB = 2
TAPS = 8
LOOKS = 128
ITERS = 8
PATCH = 32
LANES = 128
EPSILON = 1e-06
SHRINK = 0.05
F32 = jnp.float32
BF16 = jnp.bfloat16


def ceil_to(value, step):
    return -(-value // step) * step


def filter_tables(chunks):
    def pair(span):
        index = np.arange(span)
        product = (index[:, None] % PATCH) * (index[None, :] % PATCH) % PATCH
        angle = product.astype(np.float32) * np.float32(2.0 * math.pi / PATCH)
        inside = index[:, None] // PATCH == index[None, :] // PATCH
        return np.where(inside, np.cos(angle), 0.0), np.where(inside, np.sin(angle), 0.0)

    cosine, sine = pair(LANES)
    line_cos, line_sin = pair(PATCH)
    eye = np.eye(chunks)
    forward = np.block([[cosine, -sine], [sine, cosine]])
    inverse = np.block([[cosine, sine], [-sine, cosine]])
    lines = np.concatenate([np.kron(line_cos, eye), np.kron(line_sin, eye)], axis=1)
    return tuple(t.astype(ml_dtypes.bfloat16) for t in (forward, lines, inverse))


def dot(a, b, **kw):
    return jnp.dot(a, b, preferred_element_type=F32, **kw)


def turned(v):
    half = v.shape[0] // 2
    return jnp.concatenate([-v[half:], v[:half]], axis=0)


def resample_and_merge(x, taps, drifts, seams, prior, lines, xp, stage, send):
    bursts, _, sweeps, cells = x.shape[1:]
    depth = xp.shape[1] // 2
    chunks = cells // LANES
    xp[...] = jnp.zeros_like(xp)
    for b in range(bursts):
        for c in range(2):
            xp[b, c * depth : c * depth + sweeps, LANES : LANES + cells] = x[0, b, c].astype(F32)
    weights = taps[0].astype(F32)
    apart = (
        lax.broadcasted_iota(jnp.int32, (3 * LANES, LANES), 0)
        - lax.broadcasted_iota(jnp.int32, (3 * LANES, LANES), 1)
        - LANES
        + (TAPS // 2 - 1)
    )
    resampled = []
    for b in range(bursts):
        distance = apart - drifts[0, b]
        band = jnp.zeros((3 * LANES, LANES), F32)
        for k in range(TAPS):
            band = jnp.where(distance == k, weights[b : b + 1, k : k + 1], band)
        left = jnp.concatenate(
            [xp[b, :, k * LANES : (k + 3) * LANES] for k in range(chunks)], axis=0
        ).astype(BF16)
        resampled.append(dot(left, band.astype(BF16)).astype(BF16))
    columns = [
        jnp.concatenate(
            [r[(k * 2 + c) * depth : (k * 2 + c + 1) * depth] for r in resampled], axis=0
        )
        for c in range(2)
        for k in range(chunks)
    ]
    rows = send.shape[0]
    line = lax.broadcasted_iota(jnp.int32, (rows, bursts * depth), 0) - 1
    sweep = lax.broadcasted_iota(jnp.int32, (rows, bursts * depth), 1)
    place = jnp.zeros((rows, bursts * depth), F32)
    start = -prior[0]
    for b in range(bursts):
        if b > 0:
            start = start + sweeps - seams[0, b - 1]
        own = sweep - b * depth
        ramp = jnp.ones((rows, bursts * depth), F32)
        if b > 0:
            shared = jnp.full((1, 1), seams[0, b - 1] + 1, jnp.int32).astype(F32)
            ramp = ramp * jnp.clip((line - start + 1).astype(F32) / shared, 0.0, 1.0)
        if b < bursts - 1:
            shared = jnp.full((1, 1), seams[0, b] + 1, jnp.int32).astype(F32)
            ramp = ramp * jnp.clip((start + sweeps - line).astype(F32) / shared, 0.0, 1.0)
        here = (line == start + own) & (own >= 0) & (own < sweeps) & (line >= 0) & (line < lines)
        place = jnp.where(here, ramp, place)
    merged = dot(place.astype(BF16), jnp.concatenate(columns, axis=1))
    width = 2 * chunks
    for j in range(width):
        stage[pl.ds(j, rows, stride=width), :] = merged[:, j * LANES : (j + 1) * LANES]
    send[...] = stage[...].astype(BF16).reshape(send.shape)


def link(dates, frames, arrived, table, table16, gram, stage, send):
    windows = frames.shape[0]
    local_lines = arrived.shape[1]
    chunks = arrived.shape[2] // 2
    both = 2 * dates
    small = dates <= 16

    def spread(d, carry):
        for l in range(local_lines):
            half, base = l // (local_lines // 2), (l % (local_lines // 2)) * chunks
            tile = arrived[d, l].astype(F32)
            for c in range(2):
                table[half, pl.ds(base * both + c * dates + d, chunks, stride=both), :] = tile[
                    c * chunks : (c + 1) * chunks
                ]
        return carry

    lax.fori_loop(0, dates, spread, 0, unroll=small)
    for half in range(2):
        table16[:, half * LANES : (half + 1) * LANES] = table[half].astype(BF16)
    groups = local_lines // 2 * chunks
    extent = groups * LANES
    cell = lax.broadcasted_iota(jnp.int32, (2 * LANES, LOOKS), 0)

    def look(w, carry):
        frame = frames[pl.ds(w, 1), :]
        high = (frame >= extent).astype(jnp.int32)
        rest = frame - high * extent
        low = (rest & (LANES - 1)) + high * LANES
        group = rest >> 7
        hot = jnp.where(cell == low, 1.0, 0.0).astype(BF16)
        if small:
            found = dot(table16[...], hot)
            z = jnp.zeros((both, LOOKS), F32)
            for g in range(groups):
                z = jnp.where(group == g, found[g * both : (g + 1) * both], z)
        else:

            def pick(g, z):
                at = pl.ds(pl.multiple_of(g * both, both), both)
                return jnp.where(group == g, dot(table16[at, :], hot), z)

            z = lax.fori_loop(0, groups, pick, jnp.zeros((both, LOOKS), F32))
        z = jnp.concatenate([z, turned(z)], axis=1).astype(BF16)
        gram[w] = lax.dot_general(z, z, (((1,), (1,)), ((), ())), preferred_element_type=F32) * (
            1.0 / LOOKS
        )
        return carry

    lax.fori_loop(0, windows, look, 0, unroll=small)
    cov = gram[...]
    shape = (1, both, both)
    eye = lax.broadcasted_iota(jnp.int32, shape, 1) == lax.broadcasted_iota(jnp.int32, shape, 2)
    diagonal = jnp.where(eye, cov, 0.0)
    root_row = lax.rsqrt(jnp.sum(diagonal, axis=1, keepdims=True) + EPSILON)
    root_col = lax.rsqrt(jnp.sum(diagonal, axis=2, keepdims=True) + EPSILON)
    gram[...] = (1.0 - SHRINK) * cov * root_col * root_row + jnp.where(eye, SHRINK, 0.0)

    def two_steps(_, v):
        for axis in (1, 2):
            u = jnp.sum(gram[...] * v, axis=axis, keepdims=True)
            norm = jnp.sum(u * u, axis=3 - axis, keepdims=True) * (1.0 / dates)
            v = u * lax.rsqrt(norm + EPSILON)
        return v

    column = lax.broadcasted_iota(jnp.int32, (windows, both, 1), 1)
    v = jnp.where(column < dates, 1.0, 0.0).astype(F32)
    v = lax.fori_loop(0, ITERS // 2, two_steps, v, unroll=small)
    linked = v.astype(BF16).astype(F32)
    for w in range(windows):
        l, k = 1 + w // chunks, w % chunks
        half, base = l // (local_lines // 2), (l % (local_lines // 2)) * chunks
        own = table[half, (base + k) * both : (base + k + 1) * both, :]
        hist = jnp.broadcast_to(linked[w], own.shape)
        turn = turned(hist)
        scale = 1.0 / math.sqrt(dates)
        real = (jnp.sum(hist * own, axis=0, keepdims=True) * scale).astype(BF16).astype(F32)
        imag = (jnp.sum(turn * own, axis=0, keepdims=True) * scale).astype(BF16).astype(F32)
        rebuilt = real * hist + imag * turn
        for c in range(2):
            stage[pl.ds(c * windows + w, dates, stride=2 * windows), :] = rebuilt[
                c * dates : (c + 1) * dates
            ]
    send[...] = stage[...].astype(BF16).reshape(send.shape)


def patch_filter(arrived, forward, lines, inverse, stage, out):
    devices, rows = arrived.shape[0], arrived.shape[1] // 2
    chunks = rows // LB
    per = PATCH // LB
    shape = (LANES, LANES)
    same = (
        lax.broadcasted_iota(jnp.int32, shape, 0) // PATCH
        == lax.broadcasted_iota(jnp.int32, shape, 1) // PATCH
    )
    ones = jnp.where(same, 1.0 / (PATCH * PATCH), 0.0).astype(F32)

    def crossed(pair, sign):
        first, second = pair[:, :LANES], pair[:, LANES:]
        flipped = [second, -first] if sign > 0 else [-second, first]
        return jnp.concatenate([pair, jnp.concatenate(flipped, axis=1)], axis=0).astype(BF16)

    for p in range(devices // per):
        block = arrived[p * per : (p + 1) * per]
        image = jnp.concatenate(
            [block[:, c * rows : (c + 1) * rows].reshape(per * rows, LANES) for c in range(2)],
            axis=1,
        )
        first = dot(image, forward[...])
        spectrum = dot(lines[...], crossed(first, 1))
        real = spectrum[:, :LANES].reshape(PATCH, chunks, LANES)
        imag = spectrum[:, LANES:].reshape(PATCH, chunks, LANES)
        power = real * real + imag * imag
        mean = dot(jnp.sum(power, axis=0), ones, precision=lax.Precision.HIGHEST)
        ramp = jnp.sqrt(jnp.sqrt(power * (1.0 / (mean + EPSILON))[None]))
        weighted = jnp.concatenate(
            [(part * ramp).reshape(per * rows, LANES) for part in (real, imag)], axis=1
        )
        back = dot(lines[...], crossed(weighted, -1)).astype(BF16)
        filtered = dot(back, inverse[...]) * (1.0 / (PATCH * PATCH))
        for c in range(2):
            stage[c] = filtered[:, c * LANES : (c + 1) * LANES]
            for k in range(chunks):
                out[0, c, p * PATCH : (p + 1) * PATCH, k * LANES : (k + 1) * LANES] = stage[
                    c, pl.ds(k, PATCH, stride=chunks), :
                ].astype(BF16)


def kernel(
    dates, x, taps, drifts, seams, prior, frames, forward, lines, inverse, out,
    xp, stage1, send1, got1, table, table16, gram, stage2, send2, got2, stage3,
    out_sem1, in_sem1, out_sem2, in_sem2,
):
    me = lax.axis_index("date")
    small = dates <= 16

    def others(body):
        def step(off, carry):
            body(off, lax.rem(me + off, dates), lax.rem(me + dates - off, dates))
            return carry

        lax.fori_loop(1, dates, step, 0, unroll=small)

    barrier = pltpu.get_barrier_semaphore()
    others(
        lambda off, to, _: pl.semaphore_signal(
            barrier, inc=1, device_id={"date": to}, device_id_type=pl.DeviceIdType.MESH
        )
    )
    resample_and_merge(x, taps, drifts, seams, prior, LB * dates, xp, stage1, send1)
    pl.semaphore_wait(barrier, dates - 1)

    def copy(source, target, off, to, landing, out_sem, in_sem):
        return pltpu.make_async_remote_copy(
            src_ref=source,
            dst_ref=target.at[landing],
            send_sem=out_sem.at[off],
            recv_sem=in_sem.at[landing],
            device_id={"date": to},
            device_id_type=pl.DeviceIdType.MESH,
        )

    def block(g):
        return send1.at[pl.ds(g * LB, LB + 2)]

    others(lambda off, to, _: copy(block(to), got1, off, to, me, out_sem1, in_sem1).start())
    got1[me] = send1[pl.ds(me * LB, LB + 2)]
    others(lambda off, to, src: copy(block(to), got1, off, to, src, out_sem1, in_sem1).wait_recv())
    link(dates, frames, got1, table, table16, gram, stage2, send2)
    others(lambda off, to, _: copy(send2.at[to], got2, off, to, me, out_sem2, in_sem2).start())
    got2[me] = send2[me]
    others(
        lambda off, to, src: copy(send2.at[to], got2, off, to, src, out_sem2, in_sem2).wait_recv()
    )
    patch_filter(got2, forward, lines, inverse, stage3, out)
    others(lambda off, to, _: copy(block(to), got1, off, to, me, out_sem1, in_sem1).wait_send())
    others(lambda off, to, _: copy(send2.at[to], got2, off, to, me, out_sem2, in_sem2).wait_send())


def on_device(records, taps, drifts, seams, prior, frames):
    dates = lax.axis_size("date")
    _, bursts, _, sweeps, cells = records.shape
    windows = frames.shape[0]
    chunks = cells // LANES
    lines = LB * dates
    rows = ceil_to(lines + 2, 8)
    depth = ceil_to(sweeps, 16)
    width = 2 * chunks
    both = 2 * dates
    groups = (LB + 2) // 2 * chunks
    vmem = pl.BlockSpec(memory_space=pltpu.VMEM)
    smem = pl.BlockSpec(memory_space=pltpu.SMEM)
    tables = [jnp.asarray(t) for t in filter_tables(chunks)]
    return pl.pallas_call(
        functools.partial(kernel, dates),
        out_shape=jax.ShapeDtypeStruct((1, 2, lines, cells), BF16),
        in_specs=[vmem, vmem, smem, smem, smem, vmem, vmem, vmem, vmem],
        out_specs=vmem,
        scratch_shapes=[
            pltpu.VMEM((bursts, 2 * depth, cells + 2 * LANES), F32),
            pltpu.VMEM((rows * width, LANES), F32),
            pltpu.VMEM((rows, width, LANES), BF16),
            pltpu.VMEM((dates, LB + 2, width, LANES), BF16),
            pltpu.VMEM((2, groups * both, LANES), F32),
            pltpu.VMEM((groups * both, 2 * LANES), BF16),
            pltpu.VMEM((windows, both, both), F32),
            pltpu.VMEM((both * windows, LANES), F32),
            pltpu.VMEM((dates, 2 * windows, LANES), BF16),
            pltpu.VMEM((dates, 2 * windows, LANES), BF16),
            pltpu.VMEM((2, PATCH * chunks, LANES), F32),
            pltpu.SemaphoreType.DMA((dates,)),
            pltpu.SemaphoreType.DMA((dates,)),
            pltpu.SemaphoreType.DMA((dates,)),
            pltpu.SemaphoreType.DMA((dates,)),
        ],
        compiler_params=pltpu.CompilerParams(
            collective_id=0, has_side_effects=True, vmem_limit_bytes=48 * 2**20
        ),
    )(records, taps, drifts, seams, prior, frames, *tables)


def solution(mesh):
    from jax.sharding import PartitionSpec as P

    both = ("group", "date")
    return jax.shard_map(
        on_device,
        mesh=mesh,
        in_specs=(
            P(both, None, None, None, None),
            P(both, None, None),
            P(both, None),
            P(both, None),
            P(both),
            P(both, None),
        ),
        out_specs=P(both, None, None, None),
        check_vma=False,
    )
```

time: 116 us -> 30.3 us (0.26)
  other arithmetic: 35.1 us -> 0 us
  Pallas kernels: 0 us -> 25.9 us
  matrix products: 22.4 us -> 0 us
  starting transfers between devices: 17.4 us -> 0 us
  waiting for transfers between devices: 17.1 us -> 0 us
  local copies, waits for them, and re-layouts: 19.4 us -> 3.46 us
  between operations: 3.85 us -> 0.79 us
    select_n x4 -> x0, other arithmetic: 27.1 us -> none  [the longest x2 27.1 us: regridding_tableau(): matrix = jnp.where(distance == tap_index, tap_row[tap_index], matrix)]
    pallas_call x0 -> x1, Pallas kernels: none -> 25.9 us  [on_device(): pl.pallas_call(functools.partial(kernel, dates), out_shape=jax.ShapeDtype...]
    dot_general x56 -> x0, matrix products: 22.4 us -> none  [the longest x32 11.8 us: apply_matrix(): jnp.einsum('wde,we->wd', matrix, vector, precision=lax.Precision.HIGHEST)]
    all_to_all x2 -> x0, waiting for transfers between devices: 15.7 us -> none  [the longest x1 7.89 us: on_device(): lax.all_to_all(rebuilt, 'date', split_axis=0, concat_axis=2, tiled=True)[0]]
    all_to_all x2 -> x0, starting transfers between devices: 14.6 us -> none  [the longest x1 7.39 us: on_device(): lax.all_to_all(seamed_picture[None], 'date', split_axis=2, concat_axis=0,...]
    gather x3 -> x0, local copies, waits for them, and re-layouts: 8.38 us -> none  [the longest x2 7.75 us: on_device(): jnp.take(flat, viewing_frames.reshape(-1), axis=2)]
    slice x7 -> x0, local copies, waits for them, and re-layouts: 7.17 us -> none  [the longest x2 3.62 us: regridding_tableau(): matrix = jnp.where(distance == tap_index, tap_row[tap_index], matrix)]
    unnamed x4 -> x16, local copies, waits for them, and re-layouts: 0.01 us -> 3.46 us
  transfers between devices with their start and end apart: 4 -> 0, of which waited for: 3 -> 0; matrix products, arithmetic and copies ran while one was open for 0% -> 0% of each run, Pallas kernels for 0% -> 0%
where the time goes in v1:
time: 30.3 us; the launch traced here: 30.2 us
  Pallas kernels  25.9 us (85%)
  local copies, waits for them, and re-layouts  3.46 us (11%)
  between operations  0.79 us (3%)
    pallas_call x1, Pallas kernels, on_device(): pl.pallas_call(functools.partial(kernel, dates), out_shape=jax.ShapeDtype...  25.9 us
    unnamed x16, local copies, waits for them, and re-layouts  3.46 us

profile of v1, /device:TPU:0, one launch (start us, length us, event | category | flops | bytes accessed | tf_op | source)
XLA Modules:
  0.0 30.2 jit_solution(4492852530788361149)
XLA Ops:
  0.0 0.0 copy-start
  0.7 0.0 copy-start.3
  0.7 0.0 copy-start.4
  0.7 0.0 copy-start.5
  0.7 0.0 copy-start.6
  0.7 1.0 %copy.10.x = bf16[1,3,2,13,1024]{4,3,2,1,0:T(8,128)(2,1)S(1)} copy(bf16[1,3,2,13,1024]{4,2,3,1,0:T(2,128)(2,1)} %param.9) | data formatting | bytes 319488 | tf_op args[0]
  1.7 0.0 copy-done
  1.7 0.0 copy-done.3
  1.7 0.0 copy-done.4
  1.7 0.0 copy-done.5
  1.8 0.0 copy-done.6
  1.8 0.0 copy-start.1
  1.8 0.9 %copy-done.1 = bf16[256,256]{1,0:T(8,128)(2,1)S(1)} copy-done((bf16[256,256]{1,0:T(8,128)(2,1)S(1)}, bf16[256,256]{1,0:T(8,128)(2,1)}, u32[]{:S(2)}) %copy-start.1) | copy-done | bytes 131096
  2.7 0.0 copy-start.2
  2.7 0.9 %copy-done.2 = bf16[256,256]{1,0:T(8,128)(2,1)S(1)} copy-done((bf16[256,256]{1,0:T(8,128)(2,1)S(1)}, bf16[256,256]{1,0:T(8,128)(2,1)}, u32[]{:S(2)}) %copy-start.2) | copy-done | bytes 131096
  3.6 25.9 %shard_map.91 = bf16[1,2,32,1024]{3,2,1,0:T(8,128)(2,1)S(1)} custom-call(bf16[1,3,2,13,1024]{4,3,2,1,0:T(8,128)(2,1)S(1)} %copy.10.x, bf16[1,3,8]{2,1,0:T(4,128)(2,1)S(1)} %copy-done.4, s32[1,3]{1,0:T(1,128)S(1)} %copy-done.5, s32[1,2]{1,0:T(1,128)S(1)} %copy-done.6, s32[1]{0:T(128)S(6)} %copy.12.prior, s32[16,128]{1,0:T(8,128)S(1)} %copy-done.3, ...), custom_call_target="tpu_custom_call" | custom-call | tf_op jit(solution)/shard_map/pallas_call | solution.py:304
  29.5 0.7 %copy.13 = bf16[1,2,32,1024]{3,2,1,0:T(8,128)(2,1)} copy(bf16[1,2,32,1024]{3,2,1,0:T(8,128)(2,1)S(1)} %shard_map.91) | data formatting | bytes 262144
Async XLA Ops:
  0.0 1.7 %copy-start = (bf16[256,512]{1,0:T(8,128)(2,1)S(1)}, bf16[256,512]{1,0:T(8,128)(2,1)}, u32[]{:S(2)}) copy-start(bf16[256,512]{1,0:T(8,128)(2,1)} %constant.7.clone.lines) | copy-start | bytes 786436
  0.7 1.0 %copy-start.3 = (s32[16,128]{1,0:T(8,128)S(1)}, s32[16,128]{1,0:T(8,128)}, u32[]{:S(2)}) copy-start(s32[16,128]{1,0:T(8,128)} %frames.1) | copy-start | bytes 24580
  0.7 1.0 %copy-start.4 = (bf16[1,3,8]{2,1,0:T(4,128)(2,1)S(1)}, bf16[1,3,8]{2,1,0:T(4,128)(2,1)}, u32[]{:S(2)}) copy-start(bf16[1,3,8]{2,1,0:T(4,128)(2,1)} %taps.1) | copy-start | bytes 148
  0.7 1.0 %copy-start.5 = (s32[1,3]{1,0:T(1,128)S(1)}, s32[1,3]{1,0:T(1,128)}, u32[]{:S(2)}) copy-start(s32[1,3]{1,0:T(1,128)} %drifts.1) | copy-start | bytes 40
  0.7 1.0 %copy-start.6 = (s32[1,2]{1,0:T(1,128)S(1)}, s32[1,2]{1,0:T(1,128)}, u32[]{:S(2)}) copy-start(s32[1,2]{1,0:T(1,128)} %seams.1) | copy-start | bytes 28
  1.8 0.9 %copy-start.1 = (bf16[256,256]{1,0:T(8,128)(2,1)S(1)}, bf16[256,256]{1,0:T(8,128)(2,1)}, u32[]{:S(2)}) copy-start(bf16[256,256]{1,0:T(8,128)(2,1)} %constant.8.clone.inverse) | copy-start | bytes 393220
  2.7 0.9 %copy-start.2 = (bf16[256,256]{1,0:T(8,128)(2,1)S(1)}, bf16[256,256]{1,0:T(8,128)(2,1)}, u32[]{:S(2)}) copy-start(bf16[256,256]{1,0:T(8,128)(2,1)} %constant.6.clone.forward) | copy-start | bytes 393220

commit v2 on v1

--- a/solution.py
+++ b/solution.py
@@ -52,13 +52,13 @@
 
 
 def resample_and_merge(x, taps, drifts, seams, prior, lines, xp, stage, send):
-    bursts, _, sweeps, cells = x.shape[1:]
+    bursts, sweeps, _, cells = x.shape[1:]
     depth = xp.shape[1] // 2
     chunks = cells // LANES
     xp[...] = jnp.zeros_like(xp)
     for b in range(bursts):
         for c in range(2):
-            xp[b, c * depth : c * depth + sweeps, LANES : LANES + cells] = x[0, b, c].astype(F32)
+            xp[b, c * depth : c * depth + sweeps, LANES : LANES + cells] = x[0, b, :, c, :].astype(F32)
     weights = taps[0].astype(F32)
     apart = (
         lax.broadcasted_iota(jnp.int32, (3 * LANES, LANES), 0)
@@ -239,9 +239,16 @@
 def kernel(
     dates, x, taps, drifts, seams, prior, frames, forward, lines, inverse, out,
     xp, stage1, send1, got1, table, table16, gram, stage2, send2, got2, stage3,
-    out_sem1, in_sem1, out_sem2, in_sem2,
+    out_sem1, in_sem1, out_sem2, in_sem2, held_forward, held_lines, held_inverse, table_sem,
 ):
     me = lax.axis_index("date")
+    held = (held_forward, held_lines, held_inverse)
+    fetches = [
+        pltpu.make_async_copy(source, target, table_sem.at[i])
+        for i, (source, target) in enumerate(zip((forward, lines, inverse), held))
+    ]
+    for fetch in fetches:
+        fetch.start()
     small = dates <= 16
 
     def others(body):
@@ -282,7 +289,9 @@
     others(
         lambda off, to, src: copy(send2.at[to], got2, off, to, src, out_sem2, in_sem2).wait_recv()
     )
-    patch_filter(got2, forward, lines, inverse, stage3, out)
+    for fetch in fetches:
+        fetch.wait()
+    patch_filter(got2, *held, stage3, out)
     others(lambda off, to, _: copy(block(to), got1, off, to, me, out_sem1, in_sem1).wait_send())
     others(lambda off, to, _: copy(send2.at[to], got2, off, to, me, out_sem2, in_sem2).wait_send())
 
@@ -300,11 +309,12 @@
     groups = (LB + 2) // 2 * chunks
     vmem = pl.BlockSpec(memory_space=pltpu.VMEM)
     smem = pl.BlockSpec(memory_space=pltpu.SMEM)
+    far = pl.BlockSpec(memory_space=pltpu.HBM)
     tables = [jnp.asarray(t) for t in filter_tables(chunks)]
     return pl.pallas_call(
         functools.partial(kernel, dates),
         out_shape=jax.ShapeDtypeStruct((1, 2, lines, cells), BF16),
-        in_specs=[vmem, vmem, smem, smem, smem, vmem, vmem, vmem, vmem],
+        in_specs=[vmem, vmem, smem, smem, smem, vmem, far, far, far],
         out_specs=vmem,
         scratch_shapes=[
             pltpu.VMEM((bursts, 2 * depth, cells + 2 * LANES), F32),
@@ -322,11 +332,13 @@
             pltpu.SemaphoreType.DMA((dates,)),
             pltpu.SemaphoreType.DMA((dates,)),
             pltpu.SemaphoreType.DMA((dates,)),
+            *[pltpu.VMEM(t.shape, BF16) for t in tables],
+            pltpu.SemaphoreType.DMA((len(tables),)),
         ],
         compiler_params=pltpu.CompilerParams(
-            collective_id=0, has_side_effects=True, vmem_limit_bytes=48 * 2**20
+            collective_id=0, has_side_effects=True, vmem_limit_bytes=60 * 2**20
         ),
-    )(records, taps, drifts, seams, prior, frames, *tables)
+    )(jnp.swapaxes(records, 2, 3), taps, drifts, seams, prior, frames, *tables)
 
 
 def solution(mesh):

time: 30.3 us -> 29.4 us (0.970)
  local copies, waits for them, and re-layouts: 3.46 us -> 1.57 us
  Pallas kernels: 25.9 us -> 27 us
    unnamed x16 -> x1, local copies, waits for them, and re-layouts: 3.46 us -> 1.57 us
    pallas_call x1, Pallas kernels: 25.9 us -> 27 us  [on_device(): pl.pallas_call(functools.partial(kernel, dates), out_shape=jax.ShapeDtype...]
where the time goes in v2:
time: 29.4 us; the launch traced here: 29.2 us
  Pallas kernels  27 us (92%)
  local copies, waits for them, and re-layouts  1.57 us (5%)
  between operations  0.66 us (2%)
    pallas_call x1, Pallas kernels, on_device(): pl.pallas_call(functools.partial(kernel, dates), out_shape=jax.ShapeDtype...  27 us
    unnamed x1, local copies, waits for them, and re-layouts  1.57 us

profile of v2, /device:TPU:0, one launch (start us, length us, event | category | flops | bytes accessed | tf_op | source)
XLA Modules:
  0.0 29.2 jit_solution(14014749886132730617)
XLA Ops:
  0.7 27.0 %shard_map.91 = bf16[1,2,32,1024]{3,2,1,0:T(8,128)(2,1)} custom-call(bf16[1,3,13,2,1024]{4,3,2,1,0:T(2,128)(2,1)} %bitcast.1, bf16[1,3,8]{2,1,0:T(4,128)(2,1)} %taps.1, s32[1,3]{1,0:T(1,128)} %drifts.1, s32[1,2]{1,0:T(1,128)} %seams.1, s32[1]{0:T(128)S(6)} %copy.11.prior, s32[16,128]{1,0:T(8,128)} %frames.1, bf16[256,256]{1,0:T(8,128)(2,1)} %constant.6.clone.forward, ...), custom_call_target="tpu_custom_call" | custom-call | tf_op jit(solution)/shard_map/pallas_call | solution.py:314
  27.7 1.6 %copy.12 = bf16[1,2,32,1024]{3,2,1,0:T(8,128)(2,1)} copy(bf16[1,2,32,1024]{3,2,1,0:T(8,128)(2,1)} %shard_map.91) | data formatting | bytes 262144

commit v3 on v2

--- a/solution.py
+++ b/solution.py
@@ -108,15 +108,15 @@
     send[...] = stage[...].astype(BF16).reshape(send.shape)
 
 
-def link(dates, frames, arrived, table, table16, gram, stage, send):
+def link(dates, frames, arrived, border, table, table16, gram, stage, send):
     windows = frames.shape[0]
     local_lines = arrived.shape[1]
     chunks = arrived.shape[2] // 2
     both = 2 * dates
     small = dates <= 16
 
-    def spread(d, carry):
-        for l in range(local_lines):
+    def spread(which, d, carry):
+        for l in which:
             half, base = l // (local_lines // 2), (l % (local_lines // 2)) * chunks
             tile = arrived[d, l].astype(F32)
             for c in range(2):
@@ -125,7 +125,11 @@
                 ]
         return carry
 
-    lax.fori_loop(0, dates, spread, 0, unroll=small)
+    inner = functools.partial(spread, range(1, local_lines - 1))
+    outer = functools.partial(spread, (0, local_lines - 1))
+    lax.fori_loop(0, dates, inner, 0, unroll=small)
+    border()
+    lax.fori_loop(0, dates, outer, 0, unroll=small)
     for half in range(2):
         table16[:, half * LANES : (half + 1) * LANES] = table[half].astype(BF16)
     groups = local_lines // 2 * chunks
@@ -240,6 +244,7 @@
     dates, x, taps, drifts, seams, prior, frames, forward, lines, inverse, out,
     xp, stage1, send1, got1, table, table16, gram, stage2, send2, got2, stage3,
     out_sem1, in_sem1, out_sem2, in_sem2, held_forward, held_lines, held_inverse, table_sem,
+    edge_out, edge_in,
 ):
     me = lax.axis_index("date")
     held = (held_forward, held_lines, held_inverse)
@@ -267,10 +272,13 @@
     resample_and_merge(x, taps, drifts, seams, prior, LB * dates, xp, stage1, send1)
     pl.semaphore_wait(barrier, dates - 1)
 
+    def landed(target, at):
+        return target.at[at, pl.ds(1, LB)] if target is got1 else target.at[at]
+
     def copy(source, target, off, to, landing, out_sem, in_sem):
         return pltpu.make_async_remote_copy(
             src_ref=source,
-            dst_ref=target.at[landing],
+            dst_ref=landed(target, landing),
             send_sem=out_sem.at[off],
             recv_sem=in_sem.at[landing],
             device_id={"date": to},
@@ -278,12 +286,38 @@
         )
 
     def block(g):
-        return send1.at[pl.ds(g * LB, LB + 2)]
+        return send1.at[pl.ds(g * LB + 1, LB)]
 
     others(lambda off, to, _: copy(block(to), got1, off, to, me, out_sem1, in_sem1).start())
-    got1[me] = send1[pl.ds(me * LB, LB + 2)]
+    got1[me, 1 : LB + 1] = send1[pl.ds(me * LB + 1, LB)]
     others(lambda off, to, src: copy(block(to), got1, off, to, src, out_sem1, in_sem1).wait_recv())
-    link(dates, frames, got1, table, table16, gram, stage2, send2)
+
+    def edge(way):
+        line, landing = (LB, 0) if way else (1, LB + 1)
+        to = me + 1 if way else me - 1
+        return pltpu.make_async_remote_copy(
+            src_ref=got1.at[:, pl.ds(line, 1)],
+            dst_ref=got1.at[:, pl.ds(landing, 1)],
+            send_sem=edge_out.at[way],
+            recv_sem=edge_in.at[way],
+            device_id={"date": to},
+            device_id_type=pl.DeviceIdType.MESH,
+        )
+
+    first, last = me == 0, me == dates - 1
+    pl.when(jnp.logical_not(last))(lambda: edge(1).start())
+    pl.when(jnp.logical_not(first))(lambda: edge(0).start())
+
+    def blank(line):
+        got1[:, line : line + 1] = jnp.zeros((dates, 1, *got1.shape[2:]), BF16)
+
+    def border():
+        pl.when(first)(lambda: blank(0))
+        pl.when(last)(lambda: blank(LB + 1))
+        pl.when(jnp.logical_not(first))(lambda: edge(1).wait_recv())
+        pl.when(jnp.logical_not(last))(lambda: edge(0).wait_recv())
+
+    link(dates, frames, got1, border, table, table16, gram, stage2, send2)
     others(lambda off, to, _: copy(send2.at[to], got2, off, to, me, out_sem2, in_sem2).start())
     got2[me] = send2[me]
     others(
@@ -293,6 +327,8 @@
         fetch.wait()
     patch_filter(got2, *held, stage3, out)
     others(lambda off, to, _: copy(block(to), got1, off, to, me, out_sem1, in_sem1).wait_send())
+    pl.when(jnp.logical_not(last))(lambda: edge(1).wait_send())
+    pl.when(jnp.logical_not(first))(lambda: edge(0).wait_send())
     others(lambda off, to, _: copy(send2.at[to], got2, off, to, me, out_sem2, in_sem2).wait_send())
 
 
@@ -334,6 +370,8 @@
             pltpu.SemaphoreType.DMA((dates,)),
             *[pltpu.VMEM(t.shape, BF16) for t in tables],
             pltpu.SemaphoreType.DMA((len(tables),)),
+            pltpu.SemaphoreType.DMA((2,)),
+            pltpu.SemaphoreType.DMA((2,)),
         ],
         compiler_params=pltpu.CompilerParams(
             collective_id=0, has_side_effects=True, vmem_limit_bytes=60 * 2**20

time: 29.4 us -> 28.8 us (0.980)
  Pallas kernels: 27 us -> 26.4 us
    pallas_call x1, Pallas kernels: 27 us -> 26.4 us  [on_device(): pl.pallas_call(functools.partial(kernel, dates), out_shape=jax.ShapeDtype...]
where the time goes in v3:
time: 28.8 us; the launch traced here: 28.6 us
  Pallas kernels  26.4 us (92%)
  local copies, waits for them, and re-layouts  1.57 us (5%)
  between operations  0.66 us (2%)
    pallas_call x1, Pallas kernels, on_device(): pl.pallas_call(functools.partial(kernel, dates), out_shape=jax.ShapeDtype...  26.4 us
    unnamed x1, local copies, waits for them, and re-layouts  1.57 us

profile of v3, /device:TPU:0, one launch (start us, length us, event | category | flops | bytes accessed | tf_op | source)
XLA Modules:
  0.0 28.6 jit_solution(12174007253355632966)
XLA Ops:
  0.7 26.4 %shard_map.91 = bf16[1,2,32,1024]{3,2,1,0:T(8,128)(2,1)} custom-call(bf16[1,3,13,2,1024]{4,3,2,1,0:T(2,128)(2,1)} %bitcast.1, bf16[1,3,8]{2,1,0:T(4,128)(2,1)} %taps.1, s32[1,3]{1,0:T(1,128)} %drifts.1, s32[1,2]{1,0:T(1,128)} %seams.1, s32[1]{0:T(128)S(6)} %copy.11.prior, s32[16,128]{1,0:T(8,128)} %frames.1, bf16[256,256]{1,0:T(8,128)(2,1)} %constant.6.clone.forward, ...), custom_call_target="tpu_custom_call" | custom-call | tf_op jit(solution)/shard_map/pallas_call | solution.py:350
  27.1 1.6 %copy.12 = bf16[1,2,32,1024]{3,2,1,0:T(8,128)(2,1)} copy(bf16[1,2,32,1024]{3,2,1,0:T(8,128)(2,1)} %shard_map.91) | data formatting | bytes 262144

commit v4 on v3

--- a/solution.py
+++ b/solution.py
@@ -257,11 +257,12 @@
     small = dates <= 16
 
     def others(body):
-        def step(off, carry):
+        def step(j, carry):
+            off = dates // 2 + (2 * (j % 2) - 1) * ((j + 1) // 2)
             body(off, lax.rem(me + off, dates), lax.rem(me + dates - off, dates))
             return carry
 
-        lax.fori_loop(1, dates, step, 0, unroll=small)
+        lax.fori_loop(0, dates - 1, step, 0, unroll=small)
 
     barrier = pltpu.get_barrier_semaphore()
     others(
@@ -374,7 +375,7 @@
             pltpu.SemaphoreType.DMA((2,)),
         ],
         compiler_params=pltpu.CompilerParams(
-            collective_id=0, has_side_effects=True, vmem_limit_bytes=60 * 2**20
+            collective_id=0, has_side_effects=True, vmem_limit_bytes=55000 * 2**10
         ),
     )(jnp.swapaxes(records, 2, 3), taps, drifts, seams, prior, frames, *tables)
 

time: 28.8 us -> 30 us (1.042)
  Pallas kernels: 26.4 us -> 27 us
  local copies, waits for them, and re-layouts: 1.57 us -> 2.01 us
    pallas_call x1, Pallas kernels: 26.4 us -> 27 us  [on_device(): pl.pallas_call(functools.partial(kernel, dates), out_shape=jax.ShapeDtype...]
    unnamed x1 -> x9, local copies, waits for them, and re-layouts: 1.57 us -> 2.01 us
where the time goes in v4:
time: 30 us; the launch traced here: 29.7 us
  Pallas kernels  27 us (90%)
  local copies, waits for them, and re-layouts  2.01 us (7%)
  between operations  0.7 us (2%)
    pallas_call x1, Pallas kernels, on_device(): pl.pallas_call(functools.partial(kernel, dates), out_shape=jax.ShapeDtype...  27 us
    unnamed x9, local copies, waits for them, and re-layouts  2.01 us

profile of v4, /device:TPU:0, one launch (start us, length us, event | category | flops | bytes accessed | tf_op | source)
XLA Modules:
  0.0 29.7 jit_solution(12598562329400658460)
XLA Ops:
  0.0 0.0 copy-start.3
  0.7 0.0 copy-start.1
  0.7 0.0 copy-start.2
  0.7 0.0 copy-done.3
  0.7 0.7 %copy-done.1 = bf16[1,3,8]{2,1,0:T(4,128)(2,1)S(1)} copy-done((bf16[1,3,8]{2,1,0:T(4,128)(2,1)S(1)}, bf16[1,3,8]{2,1,0:T(4,128)(2,1)}, u32[]{:S(2)}) %copy-start.1) | copy-done | bytes 72
  1.3 0.0 copy-done.2
  1.4 0.0 copy-start
  1.4 0.7 %copy-done = s32[16,128]{1,0:T(8,128)S(1)} copy-done((s32[16,128]{1,0:T(8,128)S(1)}, s32[16,128]{1,0:T(8,128)}, u32[]{:S(2)}) %copy-start) | copy-done | bytes 8216
  2.0 27.0 %shard_map.91 = bf16[1,2,32,1024]{3,2,1,0:T(8,128)(2,1)S(1)} custom-call(bf16[1,3,13,2,1024]{4,3,2,1,0:T(2,128)(2,1)} %bitcast.1, bf16[1,3,8]{2,1,0:T(4,128)(2,1)S(1)} %copy-done.1, s32[1,3]{1,0:T(1,128)S(1)} %copy-done.2, s32[1,2]{1,0:T(1,128)S(1)} %copy-done.3, s32[1]{0:T(128)S(6)} %copy.11.prior, s32[16,128]{1,0:T(8,128)S(1)} %copy-done, ...), custom_call_target="tpu_custom_call" | custom-call | tf_op jit(solution)/shard_map/pallas_call | solution.py:351
  29.1 0.7 %copy.12 = bf16[1,2,32,1024]{3,2,1,0:T(8,128)(2,1)} copy(bf16[1,2,32,1024]{3,2,1,0:T(8,128)(2,1)S(1)} %shard_map.91) | data formatting | bytes 262144
Async XLA Ops:
  0.0 0.7 %copy-start.3 = (s32[1,2]{1,0:T(1,128)S(1)}, s32[1,2]{1,0:T(1,128)}, u32[]{:S(2)}) copy-start(s32[1,2]{1,0:T(1,128)} %seams.1) | copy-start | bytes 28
  0.7 0.7 %copy-start.1 = (bf16[1,3,8]{2,1,0:T(4,128)(2,1)S(1)}, bf16[1,3,8]{2,1,0:T(4,128)(2,1)}, u32[]{:S(2)}) copy-start(bf16[1,3,8]{2,1,0:T(4,128)(2,1)} %taps.1) | copy-start | bytes 148
  0.7 0.7 %copy-start.2 = (s32[1,3]{1,0:T(1,128)S(1)}, s32[1,3]{1,0:T(1,128)}, u32[]{:S(2)}) copy-start(s32[1,3]{1,0:T(1,128)} %drifts.1) | copy-start | bytes 40
  1.4 0.7 %copy-start = (s32[16,128]{1,0:T(8,128)S(1)}, s32[16,128]{1,0:T(8,128)}, u32[]{:S(2)}) copy-start(s32[16,128]{1,0:T(8,128)} %frames.1) | copy-start | bytes 24580
